TPU v7x, 128 devices: a whole 4x4x4 slice. The times are simulated.
128 devices in a mesh: pipe: 4 (over z_hi, core), expert: 32 (over x, y, z_lo).
Axes of the slice: x: 4, y: 4, z: 4 (z_hi: 2, z_lo: 2; z = z_hi * 2 + z_lo), core: 2. Of those that a mesh axis runs over, the one named last changes fastest.
Arguments:
- layer_input: bfloat16 [4, 4096, 7168], P('pipe', 'expert'), may hold values from -6 to 6
- out_grad: bfloat16 [4, 4096, 7168], P('pipe', 'expert'), may hold values from -6 to 6
- route_ids: int32 [4, 4096, 8], P('pipe', 'expert'), may hold values from 0 to 255, as said below
- route_gates: float32 [4, 4096, 8], P('pipe', 'expert'), may hold values from 0.2 to 1.2
- gate_weight: bfloat16 [4, 32, 7168, 256], P('pipe', 'expert'), may hold values from -0.0625 to 0.0625
- up_weight: bfloat16 [4, 32, 7168, 256], P('pipe', 'expert'), may hold values from -0.0625 to 0.0625
- down_weight: bfloat16 [4, 32, 256, 7168], P('pipe', 'expert'), may hold values from -0.125 to 0.125
- head_grad: bfloat16 [4096, 7168], P('expert'), may hold values from -6 to 6
Outputs:
- next_grad: bfloat16 [4, 4096, 7168], P('pipe', 'expert')
- gate_grad: float32 [4, 4096, 8], P('pipe', 'expert')
Inputs may be any that keep to these rules, and one draw needn't show every extreme that they name: `route_ids`: ids of one token are distinct. In each section and in the rows of one device, at most 16 tokens name any one expert below 4; in each section some such expert is named by exactly 16 tokens in the rows of every device.
All inputs are finite; a program needn't handle non-finite values.
Results may differ from a plain program's by a relative error of at most 0.0059.
Values may be sent and summed in bfloat16 or wider, within the bound.
No kernel may reach another device: no remote copies, remote signals or barrier semaphores. Data moves between devices by JAX's collectives and lax.ppermute only.
A program may use at most 128 MiB of HBM per device.

v0:
```python
import jax
import jax.numpy as jnp
from jax import lax
from jax.sharding import PartitionSpec as P

SLICES = 8
CAP = 16


def passed_along(block, axis, distance):
    devices = range(lax.axis_size(axis))
    route = [(i - distance, i) for i in devices if i - distance in devices]
    return lax.ppermute(block, axis, route)


def slice_backward(rows_in, rows_grad, gate_mat, up_mat, down_mat):
    gate_pre = jnp.dot(rows_in, gate_mat, preferred_element_type=jnp.float32)
    up_pre = jnp.dot(rows_in, up_mat, preferred_element_type=jnp.float32)
    sigma = jax.nn.sigmoid(gate_pre)
    swish = gate_pre * sigma
    hidden = swish * up_pre
    hidden_grad = lax.dot_general(
        rows_grad, down_mat, (((1,), (1,)), ((), ())), preferred_element_type=jnp.float32
    )
    score = jnp.sum(hidden * hidden_grad, axis=1)
    gate_back = (hidden_grad * up_pre * sigma * (1.0 + gate_pre * (1.0 - sigma))).astype(
        jnp.bfloat16
    )
    up_back = (hidden_grad * swish).astype(jnp.bfloat16)
    term = lax.dot_general(
        gate_back, gate_mat, (((1,), (1,)), ((), ())), preferred_element_type=jnp.float32
    )
    term = term + lax.dot_general(
        up_back, up_mat, (((1,), (1,)), ((), ())), preferred_element_type=jnp.float32
    )
    return (term.astype(jnp.bfloat16), score.astype(jnp.bfloat16))


def body(
    layer_input, out_grad, route_ids, route_gates, gate_weight, up_weight, down_weight, head_grad
):
    devices = lax.axis_size("expert")
    groups = devices // SLICES
    tokens = layer_input[0]
    grads = out_grad[0]
    routes = route_ids[0]
    gates = route_gates[0]
    gate_mat = gate_weight[0, 0]
    up_mat = up_weight[0, 0]
    down_mat = down_weight[0, 0]
    width = tokens.shape[1]
    named = routes[:, :, None] == jnp.arange(groups, dtype=jnp.int32)[None, None, :]
    hits = jnp.any(named, axis=1).astype(jnp.int32)
    places = jnp.cumsum(hits, axis=0) - hits
    chosen = (places[:, :, None] == jnp.arange(CAP, dtype=jnp.int32)) & (hits[:, :, None] == 1)
    picker = chosen.astype(jnp.bfloat16)
    token_rows = jnp.einsum(
        "tec,td->ecd", picker, tokens, preferred_element_type=jnp.float32
    ).astype(jnp.bfloat16)
    grad_rows = jnp.einsum("tec,td->ecd", picker, grads, preferred_element_type=jnp.float32).astype(
        jnp.bfloat16
    )
    send_in = jnp.repeat(token_rows, SLICES, axis=0)
    send_grad = jnp.repeat(grad_rows, SLICES, axis=0)
    rows_in = lax.all_to_all(send_in, "expert", split_axis=0, concat_axis=0, tiled=True)
    rows_grad = lax.all_to_all(send_grad, "expert", split_axis=0, concat_axis=0, tiled=True)
    leading = rows_in.shape[:2]
    term, score = slice_backward(
        rows_in.reshape(-1, width), rows_grad.reshape(-1, width), gate_mat, up_mat, down_mat
    )
    partial_value = term.reshape(leading + (width,))
    scores = score.reshape(leading)
    back_terms, back_scores = (
        lax.all_to_all(partial_value, "expert", split_axis=0, concat_axis=0, tiled=True),
        lax.all_to_all(scores, "expert", split_axis=0, concat_axis=0, tiled=True),
    )
    sums = jnp.sum(back_terms.astype(jnp.float32).reshape(groups, SLICES, CAP, width), axis=1)
    totals = jnp.sum(back_scores.astype(jnp.float32).reshape(groups, SLICES, CAP), axis=1)
    weighted_gate = jnp.sum(gates[:, :, None] * named.astype(jnp.float32), axis=1)
    chosen_float = chosen.astype(jnp.float32)
    mixing = chosen_float * weighted_gate[:, :, None]
    moe_grad = jnp.einsum("tec,ecd->td", mixing, sums, precision=lax.Precision.HIGHEST)
    passed = (grads.astype(jnp.float32) + moe_grad).astype(jnp.bfloat16)
    shifted = passed_along(passed, "pipe", -1)
    last_section = lax.axis_index("pipe") == lax.axis_size("pipe") - 1
    next_grad = jnp.where(last_section, head_grad, shifted)
    token_scores = jnp.einsum("tec,ec->te", chosen_float, totals, precision=lax.Precision.HIGHEST)
    gate_grad = jnp.sum(named.astype(jnp.float32) * token_scores[:, None, :], axis=2)
    return (next_grad[None], gate_grad[None])


def solution(mesh):
    in_specs = (
        P("pipe", "expert", None),
        P("pipe", "expert", None),
        P("pipe", "expert", None),
        P("pipe", "expert", None),
        P("pipe", "expert", None, None),
        P("pipe", "expert", None, None),
        P("pipe", "expert", None, None),
        P("expert", None),
    )
    out_specs = (P("pipe", "expert", None), P("pipe", "expert", None))
    return jax.shard_map(body, mesh=mesh, in_specs=in_specs, out_specs=out_specs, check_vma=False)
```

profile of v0, /device:TPU:1, one launch (start us, length us, event | category | flops | bytes accessed | tf_op | source)
XLA Modules:
  0.0 448.7 jit_solution(12885920104348764637)
XLA Ops:
  0.6 0.0 copy-start
  0.6 0.8 fusion.29
  1.5 0.1 copy.28
  1.6 0.2 reduce_window_sum.11
  1.8 0.1 copy.29
  1.8 0.3 copy-done
  2.2 0.4 convolution_convert_fusion
  2.6 3.9 broadcast_in_dim.9
  6.5 0.0 copy-start.2
  6.5 9.5 %all-to-all-start.1 = ((bf16[32,16,7168]{2,1,0:T(8,128)(2,1)}), bf16[32,16,7168]{2,1,0:T(8,128)(2,1)}, u32[]{:S(2)}, u32[]{:S(2)}) async-start(bf16[32,16,7168]{2,1,0:T(8,128)(2,1)} %bitcast.60), calls=%async_computation.1 | async-start | bytes 14680064 | tf_op jit(solution)/shard_map/all_to_all | solution.py:65
  15.9 0.0 copy-done.2
  16.0 0.4 convolution_convert_fusion.1
  16.4 119.6 %all-to-all-done.1 = bf16[32,16,7168]{2,1,0:T(8,128)(2,1)} async-done(((bf16[32,16,7168]{2,1,0:T(8,128)(2,1)}), bf16[32,16,7168]{2,1,0:T(8,128)(2,1)}, u32[]{:S(2)}, u32[]{:S(2)}) %all-to-all-start.1) | async-done | bytes 7340064 | tf_op jit(solution)/shard_map/all_to_all | solution.py:65
  135.9 3.8 broadcast_in_dim.8
  139.7 9.1 %all-to-all-start = ((bf16[32,16,7168]{2,1,0:T(8,128)(2,1)}), bf16[32,16,7168]{2,1,0:T(8,128)(2,1)}, u32[]{:S(2)}, u32[]{:S(2)}) async-start(bf16[32,16,7168]{2,1,0:T(8,128)(2,1)} %bitcast.59), calls=%async_computation | async-start | bytes 14680064 | tf_op jit(solution)/shard_map/all_to_all | solution.py:66
  148.8 0.0 copy-start.4
  148.9 6.4 %fusion.4 = f32[512,256]{0,1:T(8,128)S(1)} fusion(bf16[512,7168]{1,0:T(8,128)(2,1)} %bitcast.10, bf16[1,1,7168,256]{3,2,1,0:T(8,128)(2,1)} %param.12), kind=kOutput, calls=%fused_computation.9 | convolution fusion | flops 1879048192 | bytes 11534336 | tf_op jit(solution)/shard_map/dot_general | solution.py:17
  155.2 0.0 copy-done.4
  155.2 5.2 %fusion.7 = f32[512,256]{0,1:T(8,128)S(1)} fusion(bf16[512,7168]{1,0:T(8,128)(2,1)} %bitcast.10, bf16[1,1,7168,256]{3,2,1,0:T(8,128)(2,1)S(1)} %copy-done.4), kind=kOutput, calls=%fused_computation.12 | convolution fusion | flops 1879048192 | bytes 11534336 | tf_op jit(solution)/shard_map/dot_general | solution.py:18
  160.5 93.4 %all-to-all-done = bf16[32,16,7168]{2,1,0:T(8,128)(2,1)} async-done(((bf16[32,16,7168]{2,1,0:T(8,128)(2,1)}), bf16[32,16,7168]{2,1,0:T(8,128)(2,1)}, u32[]{:S(2)}, u32[]{:S(2)}) %all-to-all-start) | async-done | bytes 7340064 | tf_op jit(solution)/shard_map/all_to_all | solution.py:66
  253.9 0.0 copy-start.5
  253.9 6.4 %multiply_reduce_fusion = (bf16[512]{0:T(512)(128)(2,1)S(1)}, f32[512,256]{0,1:T(8,128)S(1)}) fusion(f32[512,256]{0,1:T(8,128)S(1)} %fusion.7, f32[512,256]{0,1:T(8,128)S(1)} %fusion.4, bf16[512,7168]{1,0:T(8,128)(2,1)} %bitcast.5, bf16[1,1,256,7168]{3,2,1,0:T(8,128)(2,1)} %param.14), kind=kOutput, calls=%fused_computation.19 | convolution fusion | flops 1879965184 | bytes 12583936 | tf_op jit(solution)/shard_map/dot_general | solution.py:22
  260.4 0.0 copy-done.5
  260.4 7.5 %fusion.2 = f32[512,7168]{1,0:T(8,128)} fusion(bf16[1,1,7168,256]{3,2,1,0:T(8,128)(2,1)S(1)} %copy-done.5, f32[512,256]{0,1:T(8,128)S(1)} %fusion.4, f32[512,256]{0,1:T(8,128)S(1)} %get-tuple-element.7, f32[512,256]{0,1:T(8,128)S(1)} %fusion.7), kind=kOutput, calls=%fused_computation.7 | convolution fusion | flops 1880358912 | bytes 19922944 | tf_op jit(solution)/shard_map/dot_general | solution.py:30
  267.9 0.7 convert_element_type.78
  268.6 11.0 %all-to-all-start.3 = ((bf16[32,1,16]{2,1,0:T(2,128)(2,1)}), bf16[32,1,16]{2,1,0:T(2,128)(2,1)S(1)}, u32[]{:S(2)}, u32[]{:S(2)}) async-start(bf16[32,1,16]{2,1,0:T(2,128)(2,1)} %convert_element_type.78), calls=%async_computation.3 | async-start | bytes 32768 | tf_op jit(solution)/shard_map/all_to_all | solution.py:75
  279.6 11.4 %add_convert_fusion = bf16[512,7168]{1,0:T(8,128)(2,1)} fusion(f32[512,7168]{1,0:T(8,128)} %fusion.2, bf16[1,1,7168,256]{3,2,1,0:T(8,128)(2,1)} %param.13, f32[512,256]{0,1:T(8,128)S(1)} %get-tuple-element.7, f32[512,256]{0,1:T(8,128)S(1)} %fusion.4), kind=kOutput, calls=%fused_computation.1 | convolution fusion | flops 1887174656 | bytes 26738688 | tf_op jit(solution)/shard_map/dot_general | solution.py:33
  291.0 0.0 all-to-all-done.3
  291.0 0.0 copy-start.6
  291.0 0.0 copy-start.7
  291.0 8.0 %all-to-all-start.2 = ((bf16[32,16,7168]{2,1,0:T(8,128)(2,1)}), bf16[32,16,7168]{2,1,0:T(8,128)(2,1)}, u32[]{:S(2)}, u32[]{:S(2)}) async-start(bf16[32,16,7168]{2,1,0:T(8,128)(2,1)} %bitcast.58), calls=%async_computation.2 | async-start | bytes 14680064 | tf_op jit(solution)/shard_map/all_to_all | solution.py:74
  299.0 0.1 fusion.18
  299.2 0.0 copy-done.6
  299.2 0.0 copy-done.7
  299.2 0.6 select_reduce_fusion
  299.8 104.4 %all-to-all-done.2 = bf16[32,16,7168]{2,1,0:T(8,128)(2,1)} async-done(((bf16[32,16,7168]{2,1,0:T(8,128)(2,1)}), bf16[32,16,7168]{2,1,0:T(8,128)(2,1)}, u32[]{:S(2)}, u32[]{:S(2)}) %all-to-all-start.2) | async-done | bytes 7340064 | tf_op jit(solution)/shard_map/all_to_all | solution.py:74
  404.2 0.0 copy-start.3
  404.2 4.7 %convert_reduce_fusion = f32[4,16,7168]{2,1,0:T(8,128)S(1)} fusion(bf16[32,16,7168]{2,1,0:T(8,128)(2,1)} %all-to-all-done.2), kind=kLoop, calls=%fused_computation | loop fusion | flops 6881280 | bytes 9175040 | tf_op jit(solution)/shard_map/reduce_sum | solution.py:77
  408.9 0.0 copy-done.3
  408.9 0.0 copy-start.1
  408.9 4.4 fusion.1
  413.2 8.2 %collective-permute-start = (bf16[128,7168]{1,0:T(8,128)(2,1)}, bf16[128,7168]{1,0:T(8,128)(2,1)}, u32[]{:S(2)}, u32[]{:S(2)}) collective-permute-start(bf16[128,7168]{1,0:T(8,128)(2,1)} %fusion.1), channel_id=1, source_target_pairs={{32,0},{64,32},{96,64},{33,1},{65,33},{97,65},{34,2},{66,34},{98,6... | collective-permute-start | bytes 5505032 | tf_op jit(solution)/shard_map/ppermute | solution.py:13
  421.5 24.3 %collective-permute-done = bf16[128,7168]{1,0:T(8,128)(2,1)} collective-permute-done((bf16[128,7168]{1,0:T(8,128)(2,1)}, bf16[128,7168]{1,0:T(8,128)(2,1)}, u32[]{:S(2)}, u32[]{:S(2)}) %collective-permute-start) | collective-permute-done | bytes 1835040 | tf_op jit(solution)/shard_map/ppermute | solution.py:13
  445.8 2.9 select_bitcast_fusion
  448.7 0.0 copy-done.1
  (4 shorter events, 0.1 us)
Async XLA Ops:
  0.6 1.5 copy-start
  6.5 9.5 %copy-start.2 = (bf16[1,128,7168]{2,1,0:T(8,128)(2,1)S(1)}, bf16[1,128,7168]{2,1,0:T(8,128)(2,1)}, u32[]{:S(2)}) copy-start(bf16[1,128,7168]{2,1,0:T(8,128)(2,1)} %param.9) | copy-start | bytes 5505028
  6.5 129.4 %all-to-all-start.1 = ((bf16[32,16,7168]{2,1,0:T(8,128)(2,1)}), bf16[32,16,7168]{2,1,0:T(8,128)(2,1)}, u32[]{:S(2)}, u32[]{:S(2)}) async-start(bf16[32,16,7168]{2,1,0:T(8,128)(2,1)} %bitcast.60), calls=%async_computation.1 | async-start | bytes 14680064 | tf_op jit(solution)/shard_map/all_to_all | solution.py:65
  139.7 114.2 %all-to-all-start = ((bf16[32,16,7168]{2,1,0:T(8,128)(2,1)}), bf16[32,16,7168]{2,1,0:T(8,128)(2,1)}, u32[]{:S(2)}, u32[]{:S(2)}) async-start(bf16[32,16,7168]{2,1,0:T(8,128)(2,1)} %bitcast.59), calls=%async_computation | async-start | bytes 14680064 | tf_op jit(solution)/shard_map/all_to_all | solution.py:66
  148.8 6.4 %copy-start.4 = (bf16[1,1,7168,256]{3,2,1,0:T(8,128)(2,1)S(1)}, bf16[1,1,7168,256]{3,2,1,0:T(8,128)(2,1)}, u32[]{:S(2)}) copy-start(bf16[1,1,7168,256]{3,2,1,0:T(8,128)(2,1)} %param.13) | copy-start | bytes 11010052
  253.9 6.4 %copy-start.5 = (bf16[1,1,7168,256]{3,2,1,0:T(8,128)(2,1)S(1)}, bf16[1,1,7168,256]{3,2,1,0:T(8,128)(2,1)}, u32[]{:S(2)}) copy-start(bf16[1,1,7168,256]{3,2,1,0:T(8,128)(2,1)} %param.12) | copy-start | bytes 11010052
  268.6 22.4 %all-to-all-start.3 = ((bf16[32,1,16]{2,1,0:T(2,128)(2,1)}), bf16[32,1,16]{2,1,0:T(2,128)(2,1)S(1)}, u32[]{:S(2)}, u32[]{:S(2)}) async-start(bf16[32,1,16]{2,1,0:T(2,128)(2,1)} %convert_element_type.78), calls=%async_computation.3 | async-start | bytes 32768 | tf_op jit(solution)/shard_map/all_to_all | solution.py:75
  291.0 8.2 %copy-start.6 = (s32[1,128,8]{1,2,0:T(8,128)S(1)}, s32[1,128,8]{1,2,0:T(8,128)}, u32[]{:S(2)}) copy-start(s32[1,128,8]{1,2,0:T(8,128)} %param.10) | copy-start | bytes 12292
  291.0 8.2 %copy-start.7 = (f32[1,128,8]{1,2,0:T(8,128)S(1)}, f32[1,128,8]{1,2,0:T(8,128)}, u32[]{:S(2)}) copy-start(f32[1,128,8]{1,2,0:T(8,128)} %param.11) | copy-start | bytes 12292
  291.0 113.1 %all-to-all-start.2 = ((bf16[32,16,7168]{2,1,0:T(8,128)(2,1)}), bf16[32,16,7168]{2,1,0:T(8,128)(2,1)}, u32[]{:S(2)}, u32[]{:S(2)}) async-start(bf16[32,16,7168]{2,1,0:T(8,128)(2,1)} %bitcast.58), calls=%async_computation.2 | async-start | bytes 14680064 | tf_op jit(solution)/shard_map/all_to_all | solution.py:74
  404.2 4.7 %copy-start.3 = (bf16[1,128,7168]{2,1,0:T(8,128)(2,1)S(1)}, bf16[1,128,7168]{2,1,0:T(8,128)(2,1)}, u32[]{:S(2)}) copy-start(bf16[1,128,7168]{2,1,0:T(8,128)(2,1)} %param.9) | copy-start | bytes 5505028
  408.9 39.9 %copy-start.1 = (bf16[1,128,7168]{2,1,0:T(8,128)(2,1)S(1)}, bf16[1,128,7168]{2,1,0:T(8,128)(2,1)}, u32[]{:S(2)}) copy-start(bf16[1,128,7168]{2,1,0:T(8,128)(2,1)} %param.8) | copy-start | bytes 5505028
  413.2 32.6 %collective-permute-start = (bf16[128,7168]{1,0:T(8,128)(2,1)}, bf16[128,7168]{1,0:T(8,128)(2,1)}, u32[]{:S(2)}, u32[]{:S(2)}) collective-permute-start(bf16[128,7168]{1,0:T(8,128)(2,1)} %fusion.1), channel_id=1, source_target_pairs={{32,0},{64,32},{96,64},{33,1},{65,33},{97,65},{34,2},{66,34},{98,6... | collective-permute-start | bytes 5505032 | tf_op jit(solution)/shard_map/ppermute | solution.py:13
where the time goes:
time: 452 us; the launch traced here: 449 us
  waiting for transfers between devices  342 us (76%)
  starting transfers between devices  45.8 us (10%)
  matrix products  42.2 us (9%)
  other arithmetic  9.27 us (2%)
  local copies, waits for them, and re-layouts  8.96 us (2%)
    all_to_all x1, waiting for transfers between devices, body(): lax.all_to_all(send_in, 'expert', split_axis=0, concat_axis=0, tiled=True)  120 us
    all_to_all x1, waiting for transfers between devices, body(): lax.all_to_all(partial_value, 'expert', split_axis=0, concat_axis=0, tile...  104 us
    all_to_all x1, waiting for transfers between devices, body(): lax.all_to_all(send_grad, 'expert', split_axis=0, concat_axis=0, tiled=True)  93.4 us
    ppermute x1, waiting for transfers between devices, passed_along(): return lax.ppermute(block, axis, route)  24.3 us
    dot_general x1, matrix products, slice_backward(): lax.dot_general(up_back, up_mat, (((1,), (1,)), ((), ())), preferred_elem...  11.4 us
    all_to_all x1, starting transfers between devices, body(): lax.all_to_all(scores, 'expert', split_axis=0, concat_axis=0, tiled=True)  11 us
    all_to_all x1, starting transfers between devices, body(): lax.all_to_all(send_in, 'expert', split_axis=0, concat_axis=0, tiled=True)  9.47 us
    all_to_all x1, starting transfers between devices, body(): lax.all_to_all(send_grad, 'expert', split_axis=0, concat_axis=0, tiled=True)  9.09 us
  transfers between devices with their start and end apart: 5, of which 4 were waited for; matrix products, arithmetic and copies ran while one was open for 5% of the time, Pallas kernels for 0%

commit v1 on v0

v1 whole, which is shorter than its diff:
```python
import jax
import jax.numpy as jnp
from jax import lax
from jax.sharding import PartitionSpec as P

SLICES = 8
CAP = 16
NX, NY, NZ = 4, 4, 2
BLOCKS = [(dy, dz) for dz in range(NZ) for dy in range(NY)]


def place(x, y, z):
    return ((x % NX) * NY + y % NY) * NZ + z % NZ


def send(block, dx=0, dy=0, dz=0, back=0):
    route = []
    for x in range(NX):
        for y in range(NY):
            for z in range(NZ):
                route.append((place(x, y, z), place(x + dx, y + dy, z + dz)))
    if not back:
        return lax.ppermute(block, "expert", route)
    size = NX * NY * NZ
    route = [
        (p * size + i, (p - back) * size + j)
        for p in range(back, lax.axis_size("pipe"))
        for i, j in route
    ]
    return lax.ppermute(block, ("pipe", "expert"), route)


def plane_gather(first, flip):
    width = first[0].shape[-1]

    def joined(parts, s):
        return jnp.stack([part[s] for part in parts])

    rows_z = [send(part, dz=1) for part in first]
    rows_p = [send(part, dy=1) for part in first]
    rows_m = [send(part, dy=-1) for part in first]
    ins, grads = {}, {}
    for key, parts in (((0, 0), first), ((0, 1), rows_z), ((3, 0), rows_p), ((1, 0), rows_m)):
        ins[key] = joined(parts, 0)
        grads[key] = joined(parts, 1)
    ins[2, 0] = send(ins[3, 0], dy=1)
    grads[2, 0] = send(grads[1, 0], dy=-1)
    ins[3, 1] = send(ins[0, 1], dy=1)
    ins[1, 1] = send(ins[0, 1], dy=-1)
    grads[3, 1] = send(grads[3, 0], dz=1)
    grads[1, 1] = send(grads[1, 0], dz=1)
    grads[2, 1] = send(grads[2, 0], dz=1)
    ins[2, 1] = send(ins[1, 1], dy=-1) if flip else send(ins[3, 1], dy=1)
    return (
        jnp.concatenate([ins[k] for k in BLOCKS]).reshape(-1, width),
        jnp.concatenate([grads[k] for k in BLOCKS]).reshape(-1, width),
    )


def slice_backward(rows_in, rows_grad, gate_mat, up_mat, down_mat, piece):
    gate_pre = jnp.dot(rows_in, gate_mat, preferred_element_type=jnp.float32)
    up_pre = jnp.dot(rows_in, up_mat, preferred_element_type=jnp.float32)
    sigma = jax.nn.sigmoid(gate_pre)
    swish = gate_pre * sigma
    hidden = swish * up_pre
    hidden_grad = lax.dot_general(
        rows_grad, down_mat, (((1,), (1,)), ((), ())), preferred_element_type=jnp.float32
    )
    score = jnp.sum(hidden * hidden_grad, axis=1)
    gate_back = (hidden_grad * up_pre * sigma * (1.0 + gate_pre * (1.0 - sigma))).astype(
        jnp.bfloat16
    )
    up_back = (hidden_grad * swish).astype(jnp.bfloat16)
    term = lax.dot_general(
        gate_back, gate_mat, (((1,), (1,)), ((), ())), preferred_element_type=jnp.float32
    )
    term = term + lax.dot_general(
        up_back, up_mat, (((1,), (1,)), ((), ())), preferred_element_type=jnp.float32
    )
    own = jnp.arange(128, dtype=jnp.int32)[None, :] == piece
    marked = jnp.where(own, score[:, None], 0.0)
    return jnp.concatenate([term.astype(jnp.bfloat16), marked.astype(jnp.bfloat16)], axis=1)


def added(*parts):
    total = parts[0].astype(jnp.float32)
    for part in parts[1:]:
        total = total + part.astype(jnp.float32)
    return total.astype(jnp.bfloat16)


def plane_reduce(terms):
    width = terms.shape[-1]
    terms = terms.reshape(len(BLOCKS), 2, CAP, width)
    late = {k: terms[i, 0] for i, k in enumerate(BLOCKS)}
    soon = {k: terms[i, 1] for i, k in enumerate(BLOCKS)}
    cross = send(terms[NY:, 1], dz=1)
    far_p = send(late[2, 0], dy=1)
    far_m = send(late[2, 1], dy=-1)
    sums = {dy: added(soon[dy, 0], cross[dy]) for dy in range(NY)}
    near_p = send(jnp.stack([added(late[1, 0], far_p), late[1, 1]]), dy=1)
    near_m = send(jnp.stack([late[3, 0], added(late[3, 1], far_m)]), dy=-1)
    half = CAP // 2
    away_p = send(sums[2][:half], dy=1)
    away_m = send(sums[2][half:], dy=-1)
    other = added(late[0, 1], near_p[1], near_m[1])
    last = send(other, dz=1)
    next_p = send(
        jnp.concatenate([added(sums[1][:half], away_p), sums[1][half:]]), dy=1
    )
    next_m = send(
        jnp.concatenate([sums[3][:half], added(sums[3][half:], away_m)]), dy=-1
    )
    return (
        added(late[0, 0], near_p[0], near_m[0], last),
        added(sums[0], next_p, next_m),
    )


def body(
    layer_input, out_grad, route_ids, route_gates, gate_weight, up_weight, down_weight, head_grad
):
    holder = lax.axis_index("expert")
    piece = holder % SLICES
    group = holder // SLICES
    tokens = layer_input[0]
    grads = out_grad[0]
    routes = route_ids[0]
    gates = route_gates[0]
    gate_mat = gate_weight[0, 0]
    up_mat = up_weight[0, 0]
    down_mat = down_weight[0, 0]
    width = tokens.shape[1]
    order = (jnp.arange(NX, dtype=jnp.int32) + group) % NX
    named = routes[:, :, None] == order[None, None, :]
    hits = jnp.any(named, axis=1).astype(jnp.int32)
    places = jnp.cumsum(hits, axis=0) - hits
    chosen = (places[:, :, None] == jnp.arange(CAP, dtype=jnp.int32)) & (hits[:, :, None] == 1)
    picker = chosen.astype(jnp.bfloat16)
    token_rows = jnp.einsum(
        "tec,td->ecd", picker, tokens, preferred_element_type=jnp.float32
    ).astype(jnp.bfloat16)
    grad_rows = jnp.einsum("tec,td->ecd", picker, grads, preferred_element_type=jnp.float32).astype(
        jnp.bfloat16
    )
    rows = [jnp.stack([token_rows[dx], grad_rows[dx]]) for dx in range(NX)]
    arrived = [rows[0]] + [send(rows[dx], dx=dx) for dx in range(1, NX)]

    weighted_gate = jnp.sum(gates[:, :, None] * named.astype(jnp.float32), axis=1)
    chosen_float = chosen.astype(jnp.float32)
    mixing = (chosen_float * weighted_gate[:, :, None]).reshape(-1, NX * CAP)
    mixing_back = send(mixing, back=1)
    grads_back = send(grads, back=1)

    chunks = [arrived[:2], [jnp.stack([arrived[2][s], arrived[3][s]]) for s in range(2)]]
    results = []
    for c in range(2):
        if c == 0:
            ins, gs = plane_gather(arrived[:2], False)
        else:
            ins, gs = plane_gather(arrived[2:], True)
        terms = slice_backward(ins, gs, gate_mat, up_mat, down_mat, piece)
        results.extend(plane_reduce(terms))
    scores, moved = [], []
    for dx in range(NX):
        part = results[dx]
        marks = part[:, width:]
        scores.append(send(marks, dx=-dx) if dx else marks)
        moved.append(send(part[:, :width], dx=-dx, back=1))
    sums = jnp.concatenate(moved)
    high = lax.reduce_precision(mixing_back, 8, 7)
    low = mixing_back - high
    moe_grad = jnp.dot(
        high.astype(jnp.bfloat16), sums, preferred_element_type=jnp.float32
    ) + jnp.dot(low.astype(jnp.bfloat16), sums, preferred_element_type=jnp.float32)
    passed = (grads_back.astype(jnp.float32) + moe_grad).astype(jnp.bfloat16)
    last_section = lax.axis_index("pipe") == lax.axis_size("pipe") - 1
    next_grad = jnp.where(last_section, head_grad, passed)
    totals = jnp.sum(jnp.stack(scores).astype(jnp.float32), axis=2)
    token_scores = jnp.sum(chosen_float * totals[None], axis=2)
    gate_grad = jnp.sum(named.astype(jnp.float32) * token_scores[:, None, :], axis=2)
    return (next_grad[None], gate_grad[None])


def solution(mesh):
    in_specs = (
        P("pipe", "expert", None),
        P("pipe", "expert", None),
        P("pipe", "expert", None),
        P("pipe", "expert", None),
        P("pipe", "expert", None, None),
        P("pipe", "expert", None, None),
        P("pipe", "expert", None, None),
        P("expert", None),
    )
    out_specs = (P("pipe", "expert", None), P("pipe", "expert", None))
    return jax.shard_map(body, mesh=mesh, in_specs=in_specs, out_specs=out_specs, check_vma=False)
```

time: 452 us -> 335 us (0.74)
  waiting for transfers between devices: 342 us -> 201 us
  starting transfers between devices: 45.8 us -> 79.1 us
  matrix products: 42.2 us -> 30.7 us
    all_to_all x4 -> x0, waiting for transfers between devices: 317 us -> none  [the longest x1 120 us: body(): lax.all_to_all(send_in, 'expert', split_axis=0, concat_axis=0, tiled=True)]
    ppermute x1 -> x60, waiting for transfers between devices: 24.3 us -> 201 us  [the longest x54 190 us: send(): return lax.ppermute(block, 'expert', route)]
    ppermute x1 -> x60, starting transfers between devices: 8.21 us -> 79.1 us  [the longest x54 41.8 us: send(): return lax.ppermute(block, 'expert', route)]
    all_to_all x4 -> x0, starting transfers between devices: 37.6 us -> none  [the longest x1 11 us: body(): lax.all_to_all(scores, 'expert', split_axis=0, concat_axis=0, tiled=True)]
    broadcast_in_dim x2 -> x0, local copies, waits for them, and re-layouts: 7.74 us -> none  [the longest x1 3.91 us: body(): send_in = jnp.repeat(token_rows, SLICES, axis=0)]
    unnamed x16 -> x50, local copies, waits for them, and re-layouts: 0.35 us -> 6.96 us
    dot_general x1 -> x2, matrix products: 7.52 us -> 2.46 us  [slice_backward(): lax.dot_general(gate_back, gate_mat, (((1,), (1,)), ((), ())), preferred_...]
    reduce_sum x2, other arithmetic: 4.71 us -> 0.18 us  [the longest x1 0.1 us: body(): token_scores = jnp.sum(chosen_float * totals[None], axis=2)]
  transfers between devices with their start and end apart: 5 -> 60, of which waited for: 4 -> 28; matrix products, arithmetic and copies ran while one was open for 5% -> 11% of each run, Pallas kernels for 0% -> 0%
where the time goes in v1:
time: 335 us; the launch traced here: 328 us
  waiting for transfers between devices  201 us (60%)
  starting transfers between devices  79.1 us (24%)
  matrix products  30.7 us (9%)
  local copies, waits for them, and re-layouts  9.61 us (3%)
  other arithmetic  6.53 us (2%)
    ppermute x54, waiting for transfers between devices, send(): return lax.ppermute(block, 'expert', route)  190 us
    ppermute x54, starting transfers between devices, send(): return lax.ppermute(block, 'expert', route)  41.8 us
    ppermute x6, starting transfers between devices, send(): return lax.ppermute(block, ('pipe', 'expert'), route)  37.3 us
    dot_general x2, matrix products, slice_backward(): lax.dot_general(up_back, up_mat, (((1,), (1,)), ((), ())), preferred_elem...  12.2 us
    ppermute x6, waiting for transfers between devices, send(): return lax.ppermute(block, ('pipe', 'expert'), route)  10.2 us
    unnamed x50, local copies, waits for them, and re-layouts  6.96 us
  transfers between devices with their start and end apart: 60, of which 28 were waited for; matrix products, arithmetic and copies ran while one was open for 11% of the time, Pallas kernels for 0%

profile of v1, /device:TPU:1, one launch (start us, length us, event | category | flops | bytes accessed | tf_op | source)
XLA Modules:
  0.0 328.4 jit_solution(4104087160495793349)
XLA Ops:
  1.9 1.9 convolution_convert_fusion.1
  5.9 2.6 collective-permute-start.8
  8.5 1.3 collective-permute-start.6
  9.8 1.4 collective-permute-start.3
  14.0 2.4 collective-permute-start.29
  16.6 7.5 %collective-permute-done.2 = bf16[2,16,7168]{2,1,0:T(8,128)(2,1)} collective-permute-done((bf16[2,16,7168]{2,1,0:T(8,128)(2,1)}, bf16[2,16,7168]{2,1,0:T(8,128)(2,1)}, u32[]{:S(2)}, u32[]{:S(2)}) %collective-permute-start.2) | collective-permute-done | bytes 458784 | tf_op jit(solution)/shard_map/ppermute | solution.py:23
  24.1 1.3 collective-permute-start.30
  25.3 9.4 %collective-permute-done.29 = bf16[2,16,7168]{2,1,0:T(8,128)(2,1)S(1)} collective-permute-done((bf16[2,16,7168]{2,1,0:T(8,128)(2,1)}, bf16[2,16,7168]{2,1,0:T(8,128)(2,1)S(1)}, u32[]{:S(2)}, u32[]{:S(2)}) %collective-permute-start.29) | collective-permute-done | bytes 458784 | tf_op jit(solution)/shard_map/ppermute | solution.py:23
  34.8 1.9 slice_dynamic-update-slice_fusion.10
  36.7 1.3 collective-permute-start.34
  39.0 1.9 slice_dynamic-update-slice_fusion.9
  40.9 5.5 %collective-permute-start = (bf16[128,7168]{1,0:T(8,128)(2,1)}, bf16[128,7168]{1,0:T(8,128)(2,1)S(1)}, u32[]{:S(2)}, u32[]{:S(2)}) collective-permute-start(bf16[128,7168]{1,0:T(8,128)(2,1)} %bitcast), channel_id=1, source_target_pairs={{32,0},{33,1},{34,2},{35,3},{36,4},{37,5},{38,6},{39,7},{40,8},{41... | collective-permute-start | bytes 5505032 | tf_op jit(solution)/shard_map/ppermute | solution.py:30
  46.7 9.0 %collective-permute-done.34 = bf16[2,16,7168]{2,1,0:T(8,128)(2,1)S(1)} collective-permute-done((bf16[2,16,7168]{2,1,0:T(8,128)(2,1)S(1)}, bf16[2,16,7168]{2,1,0:T(8,128)(2,1)S(1)}, u32[]{:S(2)}, u32[]{:S(2)}) %collective-permute-start.34) | collective-permute-done | bytes 458784 | tf_op jit(solution)/shard_map/ppermute | solution.py:23
  55.8 9.7 %collective-permute-done.35 = bf16[2,16,7168]{2,1,0:T(8,128)(2,1)S(1)} collective-permute-done((bf16[2,16,7168]{2,1,0:T(8,128)(2,1)S(1)}, bf16[2,16,7168]{2,1,0:T(8,128)(2,1)S(1)}, u32[]{:S(2)}, u32[]{:S(2)}) %collective-permute-start.35) | collective-permute-done | bytes 458784 | tf_op jit(solution)/shard_map/ppermute | solution.py:23
  67.3 8.2 %collective-permute-done.31 = bf16[2,16,7168]{2,1,0:T(8,128)(2,1)S(1)} collective-permute-done((bf16[2,16,7168]{2,1,0:T(8,128)(2,1)S(1)}, bf16[2,16,7168]{2,1,0:T(8,128)(2,1)S(1)}, u32[]{:S(2)}, u32[]{:S(2)}) %collective-permute-start.31) | collective-permute-done | bytes 458784 | tf_op jit(solution)/shard_map/ppermute | solution.py:23
  76.4 8.3 %collective-permute-done.32 = bf16[2,16,7168]{2,1,0:T(8,128)(2,1)S(1)} collective-permute-done((bf16[2,16,7168]{2,1,0:T(8,128)(2,1)S(1)}, bf16[2,16,7168]{2,1,0:T(8,128)(2,1)S(1)}, u32[]{:S(2)}, u32[]{:S(2)}) %collective-permute-start.32) | collective-permute-done | bytes 458784 | tf_op jit(solution)/shard_map/ppermute | solution.py:23
  84.7 8.4 %collective-permute-done.13 = bf16[2,16,7168]{2,1,0:T(8,128)(2,1)S(1)} collective-permute-done((bf16[2,16,7168]{2,1,0:T(8,128)(2,1)S(1)}, bf16[2,16,7168]{2,1,0:T(8,128)(2,1)S(1)}, u32[]{:S(2)}, u32[]{:S(2)}) %collective-permute-start.13) | collective-permute-done | bytes 458784 | tf_op jit(solution)/shard_map/ppermute | solution.py:23
  93.2 1.3 collective-permute-start.5
  94.5 6.3 %collective-permute-done.5 = bf16[2,16,7168]{2,1,0:T(8,128)(2,1)S(1)} collective-permute-done((bf16[2,16,7168]{2,1,0:T(8,128)(2,1)S(1)}, bf16[2,16,7168]{2,1,0:T(8,128)(2,1)S(1)}, u32[]{:S(2)}, u32[]{:S(2)}) %collective-permute-start.5) | collective-permute-done | bytes 458784 | tf_op jit(solution)/shard_map/ppermute | solution.py:23
  100.9 8.4 %collective-permute-done.41 = bf16[2,16,7168]{2,1,0:T(8,128)(2,1)S(1)} collective-permute-done((bf16[2,16,7168]{2,1,0:T(8,128)(2,1)S(1)}, bf16[2,16,7168]{2,1,0:T(8,128)(2,1)S(1)}, u32[]{:S(2)}, u32[]{:S(2)}) %collective-permute-start.41) | collective-permute-done | bytes 458784 | tf_op jit(solution)/shard_map/ppermute | solution.py:23
  109.3 1.3 collective-permute-start.33
  110.7 6.3 %collective-permute-done.33 = bf16[2,16,7168]{2,1,0:T(8,128)(2,1)S(1)} collective-permute-done((bf16[2,16,7168]{2,1,0:T(8,128)(2,1)S(1)}, bf16[2,16,7168]{2,1,0:T(8,128)(2,1)S(1)}, u32[]{:S(2)}, u32[]{:S(2)}) %collective-permute-start.33) | collective-permute-done | bytes 458784 | tf_op jit(solution)/shard_map/ppermute | solution.py:23
  117.1 1.5 collective-permute-start.10
  119.2 5.4 %collective-permute-done.37 = bf16[2,16,7168]{2,1,0:T(8,128)(2,1)S(1)} collective-permute-done((bf16[2,16,7168]{2,1,0:T(8,128)(2,1)S(1)}, bf16[2,16,7168]{2,1,0:T(8,128)(2,1)S(1)}, u32[]{:S(2)}, u32[]{:S(2)}) %collective-permute-start.37) | collective-permute-done | bytes 458784 | tf_op jit(solution)/shard_map/ppermute | solution.py:23
  124.6 2.2 collective-permute-start.14
  126.9 2.3 collective-permute-done.10
  129.2 7.6 %collective-permute-done.38 = bf16[2,16,7168]{2,1,0:T(8,128)(2,1)S(1)} collective-permute-done((bf16[2,16,7168]{2,1,0:T(8,128)(2,1)S(1)}, bf16[2,16,7168]{2,1,0:T(8,128)(2,1)S(1)}, u32[]{:S(2)}, u32[]{:S(2)}) %collective-permute-start.38) | collective-permute-done | bytes 458784 | tf_op jit(solution)/shard_map/ppermute | solution.py:23
  136.9 1.9 collective-permute-start.42
  139.5 12.3 %collective-permute-done.11 = bf16[2,16,7168]{2,1,0:T(8,128)(2,1)S(1)} collective-permute-done((bf16[2,16,7168]{2,1,0:T(8,128)(2,1)S(1)}, bf16[2,16,7168]{2,1,0:T(8,128)(2,1)S(1)}, u32[]{:S(2)}, u32[]{:S(2)}) %collective-permute-start.11) | collective-permute-done | bytes 458784 | tf_op jit(solution)/shard_map/ppermute | solution.py:23
  152.1 7.3 %collective-permute-done.12 = bf16[2,16,7168]{2,1,0:T(8,128)(2,1)S(1)} collective-permute-done((bf16[2,16,7168]{2,1,0:T(8,128)(2,1)S(1)}, bf16[2,16,7168]{2,1,0:T(8,128)(2,1)S(1)}, u32[]{:S(2)}, u32[]{:S(2)}) %collective-permute-start.12) | collective-permute-done | bytes 458784 | tf_op jit(solution)/shard_map/ppermute | solution.py:23
  159.7 1.3 collective-permute-start.39
  161.0 1.6 collective-permute-start.43
  162.6 15.4 %collective-permute-done.39 = bf16[2,16,7168]{2,1,0:T(8,128)(2,1)S(1)} collective-permute-done((bf16[2,16,7168]{2,1,0:T(8,128)(2,1)S(1)}, bf16[2,16,7168]{2,1,0:T(8,128)(2,1)S(1)}, u32[]{:S(2)}, u32[]{:S(2)}) %collective-permute-start.39) | collective-permute-done | bytes 458784 | tf_op jit(solution)/shard_map/ppermute | solution.py:23
  178.1 8.4 %collective-permute-done.16 = bf16[2,16,7168]{2,1,0:T(8,128)(2,1)S(1)} collective-permute-done((bf16[2,16,7168]{2,1,0:T(8,128)(2,1)S(1)}, bf16[2,16,7168]{2,1,0:T(8,128)(2,1)S(1)}, u32[]{:S(2)}, u32[]{:S(2)}) %collective-permute-start.16) | collective-permute-done | bytes 458784 | tf_op jit(solution)/shard_map/ppermute | solution.py:23
  186.7 1.6 fusion.8
  188.7 1.6 fusion.14
  190.4 1.5 fusion.4
  191.9 1.5 fusion.11
  195.1 1.2 fusion.6
  198.4 3.2 multiply_reduce_fusion
  202.8 11.0 %fusion.1 = bf16[256,7168]{1,0:T(8,128)(2,1)S(1)} fusion(f32[256,7168]{1,0:T(8,128)S(1)} %fusion.2, bf16[1,1,7168,256]{3,2,1,0:T(8,128)(2,1)S(1)} %copy-done.3, f32[256,256]{0,1:T(8,128)S(1)} %get-tuple-element.87, f32[256,256]{0,1:T(8,128)S(1)} %fusion.4), kind=kOutput, calls=%fused_computation.3 | convolution fusion | flops 943587328 | bytes 15204352 | tf_op jit(solution)/shard_map/dot_general | solution.py:77
  214.9 2.7 collective-permute-start.19
  217.7 3.3 %collective-permute-done.17 = bf16[16,7296]{1,0:T(8,128)(2,1)S(1)} collective-permute-done((bf16[16,7296]{1,0:T(8,128)(2,1)S(1)}, bf16[16,7296]{1,0:T(8,128)(2,1)S(1)}, u32[]{:S(2)}, u32[]{:S(2)}) %collective-permute-start.17) | collective-permute-done | bytes 233504 | tf_op jit(solution)/shard_map/ppermute | solution.py:23
  221.9 8.1 %collective-permute-done.23 = bf16[4,16,7296]{2,1,0:T(8,128)(2,1)S(1)} collective-permute-done((bf16[4,16,7296]{2,1,0:T(8,128)(2,1)S(1)}, bf16[4,16,7296]{2,1,0:T(8,128)(2,1)S(1)}, u32[]{:S(2)}, u32[]{:S(2)}) %collective-permute-start.23) | collective-permute-done | bytes 933920 | tf_op jit(solution)/shard_map/ppermute | solution.py:23
  230.6 2.7 collective-permute-start.26
  233.3 7.2 %collective-permute-done.51 = bf16[4,16,7296]{2,1,0:T(8,128)(2,1)S(1)} collective-permute-done((bf16[4,16,7296]{2,1,0:T(8,128)(2,1)S(1)}, bf16[4,16,7296]{2,1,0:T(8,128)(2,1)S(1)}, u32[]{:S(2)}, u32[]{:S(2)}) %collective-permute-start.51) | collective-permute-done | bytes 933920 | tf_op jit(solution)/shard_map/ppermute | solution.py:23
  241.4 1.3 collective-permute-start.52
  242.7 1.6 collective-permute-start.54
  244.3 3.9 %collective-permute-done.52 = bf16[8,7296]{1,0:T(8,128)(2,1)S(1)} collective-permute-done((bf16[8,7296]{1,0:T(8,128)(2,1)S(1)}, bf16[8,7296]{1,0:T(8,128)(2,1)S(1)}, u32[]{:S(2)}, u32[]{:S(2)}) %collective-permute-start.52) | collective-permute-done | bytes 116768 | tf_op jit(solution)/shard_map/ppermute | solution.py:23
  248.2 3.8 %collective-permute-done.54 = bf16[8,7296]{1,0:T(8,128)(2,1)S(1)} collective-permute-done((bf16[8,7296]{1,0:T(8,128)(2,1)S(1)}, bf16[8,7296]{1,0:T(8,128)(2,1)S(1)}, u32[]{:S(2)}, u32[]{:S(2)}) %collective-permute-start.54) | collective-permute-done | bytes 116768 | tf_op jit(solution)/shard_map/ppermute | solution.py:23
  252.1 2.4 collective-permute-done.27
  254.5 5.1 %collective-permute-done.25 = bf16[16,7296]{1,0:T(8,128)(2,1)S(1)} collective-permute-done((bf16[16,7296]{1,0:T(8,128)(2,1)S(1)}, bf16[16,7296]{1,0:T(8,128)(2,1)S(1)}, u32[]{:S(2)}, u32[]{:S(2)}) %collective-permute-start.25) | collective-permute-done | bytes 233504 | tf_op jit(solution)/shard_map/ppermute | solution.py:23
  261.4 14.3 %collective-permute-done.55 = bf16[16,7296]{1,0:T(8,128)(2,1)S(1)} collective-permute-done((bf16[16,7296]{1,0:T(8,128)(2,1)S(1)}, bf16[16,7296]{1,0:T(8,128)(2,1)S(1)}, u32[]{:S(2)}, u32[]{:S(2)}) %collective-permute-start.55) | collective-permute-done | bytes 233504 | tf_op jit(solution)/shard_map/ppermute | solution.py:23
  276.1 1.5 collective-permute-start.59
  277.5 1.5 collective-permute-start.49
  279.0 1.9 collective-permute-done.21
  281.1 21.9 %collective-permute-start.22 = (bf16[16,7168]{1,0:T(8,128)(2,1)S(1)}, bf16[16,7168]{1,0:T(8,128)(2,1)S(1)}, u32[]{:S(2)}, u32[]{:S(2)}) collective-permute-start(bf16[16,7168]{1,0:T(8,128)(2,1)S(1)} %slice.430), channel_id=1, source_target_pairs={{32,0},{33,1},{34,2},{35,3},{36,4},{37,5},{38,6},{39,7},{40,8},{41... | collective-permute-start | bytes 688136 | tf_op jit(solution)/shard_map/ppermute | solution.py:30
  303.9 4.2 %collective-permute-start.28 = (bf16[16,7168]{1,0:T(8,128)(2,1)S(1)}, bf16[16,7168]{1,0:T(8,128)(2,1)S(1)}, u32[]{:S(2)}, u32[]{:S(2)}) collective-permute-start(bf16[16,7168]{1,0:T(8,128)(2,1)S(1)} %slice.446), channel_id=1, source_target_pairs={{32,24},{33,25},{34,26},{35,27},{36,28},{37,29},{38,30},{39,31},{4... | collective-permute-start | bytes 688136 | tf_op jit(solution)/shard_map/ppermute | solution.py:30
  308.0 1.9 collective-permute-start.56
  310.0 1.9 collective-permute-start.50
  312.9 1.9 collective-permute-start.1
  314.8 1.4 collective-permute-done.28
  316.2 8.8 %collective-permute-done.50 = bf16[16,7168]{1,0:T(8,128)(2,1)S(1)} collective-permute-done((bf16[16,7168]{1,0:T(8,128)(2,1)S(1)}, bf16[16,7168]{1,0:T(8,128)(2,1)S(1)}, u32[]{:S(2)}, u32[]{:S(2)}) %collective-permute-start.50) | collective-permute-done | bytes 229408 | tf_op jit(solution)/shard_map/ppermute | solution.py:30
  325.8 2.4 fusion.21
  (199 shorter events, 26.5 us)
Async XLA Ops:
  5.9 111.2 %collective-permute-start.8 = (bf16[2,16,7168]{2,1,0:T(8,128)(2,1)S(1)}, bf16[2,16,7168]{2,1,0:T(8,128)(2,1)S(1)}, u32[]{:S(2)}, u32[]{:S(2)}) collective-permute-start(bf16[2,16,7168]{2,1,0:T(8,128)(2,1)S(1)} %pad_maximum_fusion.7), channel_id=1, source_target_pairs={{0,1},{1,0},{2,3},{3,2},{4,5},{5,4},{6,7},{7,6},{8,9},{9,8},{10,11... | collective-permute-start | bytes 1376264 | tf_op jit(solution)/shard_map/ppermute | solution.py:23
  8.5 32.4 %collective-permute-start.6 = (bf16[2,16,7168]{2,1,0:T(8,128)(2,1)S(1)}, bf16[2,16,7168]{2,1,0:T(8,128)(2,1)S(1)}, u32[]{:S(2)}, u32[]{:S(2)}) collective-permute-start(bf16[2,16,7168]{2,1,0:T(8,128)(2,1)S(1)} %pad_maximum_fusion.7), channel_id=1, source_target_pairs={{0,2},{1,3},{2,4},{3,5},{4,6},{5,7},{6,0},{7,1},{8,10},{9,11},{10,... | collective-permute-start | bytes 1376264 | tf_op jit(solution)/shard_map/ppermute | solution.py:23
  9.8 26.9 %collective-permute-start.3 = (bf16[2,16,7168]{2,1,0:T(8,128)(2,1)S(1)}, bf16[2,16,7168]{2,1,0:T(8,128)(2,1)}, u32[]{:S(2)}, u32[]{:S(2)}) collective-permute-start(bf16[2,16,7168]{2,1,0:T(8,128)(2,1)S(1)} %pad_maximum_fusion.7), channel_id=1, source_target_pairs={{0,6},{1,7},{2,0},{3,1},{4,2},{5,3},{6,4},{7,5},{8,14},{9,15},{10,... | collective-permute-start | bytes 1376264 | tf_op jit(solution)/shard_map/ppermute | solution.py:23
  12.0 12.1 %collective-permute-start.2 = (bf16[2,16,7168]{2,1,0:T(8,128)(2,1)}, bf16[2,16,7168]{2,1,0:T(8,128)(2,1)}, u32[]{:S(2)}, u32[]{:S(2)}) collective-permute-start(bf16[2,16,7168]{2,1,0:T(8,128)(2,1)} %pad_maximum_fusion.6), channel_id=1, source_target_pairs={{0,8},{1,9},{2,10},{3,11},{4,12},{5,13},{6,14},{7,15},{8,16},{9,17... | collective-permute-start | bytes 1376264 | tf_op jit(solution)/shard_map/ppermute | solution.py:23
  14.0 20.8 %collective-permute-start.29 = (bf16[2,16,7168]{2,1,0:T(8,128)(2,1)}, bf16[2,16,7168]{2,1,0:T(8,128)(2,1)S(1)}, u32[]{:S(2)}, u32[]{:S(2)}) collective-permute-start(bf16[2,16,7168]{2,1,0:T(8,128)(2,1)} %pad_maximum_fusion.12), channel_id=1, source_target_pairs={{0,16},{1,17},{2,18},{3,19},{4,20},{5,21},{6,22},{7,23},{8,24},{9,... | collective-permute-start | bytes 1376264 | tf_op jit(solution)/shard_map/ppermute | solution.py:23
  24.1 13.9 %collective-permute-start.30 = (bf16[2,16,7168]{2,1,0:T(8,128)(2,1)S(1)}, bf16[2,16,7168]{2,1,0:T(8,128)(2,1)S(1)}, u32[]{:S(2)}, u32[]{:S(2)}) collective-permute-start(bf16[2,16,7168]{2,1,0:T(8,128)(2,1)S(1)} %pad_maximum_fusion.13), channel_id=1, source_target_pairs={{0,24},{1,25},{2,26},{3,27},{4,28},{5,29},{6,30},{7,31},{8,0},{9,1... | collective-permute-start | bytes 1376264 | tf_op jit(solution)/shard_map/ppermute | solution.py:23
  34.8 11.6 %collective-permute-start.7 = (bf16[2,16,7168]{2,1,0:T(8,128)(2,1)}, bf16[2,16,7168]{2,1,0:T(8,128)(2,1)S(1)}, u32[]{:S(2)}, u32[]{:S(2)}) collective-permute-start(bf16[2,16,7168]{2,1,0:T(8,128)(2,1)} %collective-permute-done.2), channel_id=1, source_target_pairs={{0,2},{1,3},{2,4},{3,5},{4,6},{5,7},{6,0},{7,1},{8,10},{9,11},{10,... | collective-permute-start | bytes 1376264 | tf_op jit(solution)/shard_map/ppermute | solution.py:23
  36.7 19.0 %collective-permute-start.34 = (bf16[2,16,7168]{2,1,0:T(8,128)(2,1)S(1)}, bf16[2,16,7168]{2,1,0:T(8,128)(2,1)S(1)}, u32[]{:S(2)}, u32[]{:S(2)}) collective-permute-start(bf16[2,16,7168]{2,1,0:T(8,128)(2,1)S(1)} %collective-permute-done.29), channel_id=1, source_target_pairs={{0,2},{1,3},{2,4},{3,5},{4,6},{5,7},{6,0},{7,1},{8,10},{9,11},{10,... | collective-permute-start | bytes 1376264 | tf_op jit(solution)/shard_map/ppermute | solution.py:23
  38.0 27.5 %collective-permute-start.35 = (bf16[2,16,7168]{2,1,0:T(8,128)(2,1)S(1)}, bf16[2,16,7168]{2,1,0:T(8,128)(2,1)S(1)}, u32[]{:S(2)}, u32[]{:S(2)}) collective-permute-start(bf16[2,16,7168]{2,1,0:T(8,128)(2,1)S(1)} %collective-permute-done.30), channel_id=1, source_target_pairs={{0,2},{1,3},{2,4},{3,5},{4,6},{5,7},{6,0},{7,1},{8,10},{9,11},{10,... | collective-permute-start | bytes 1376264 | tf_op jit(solution)/shard_map/ppermute | solution.py:23
  40.9 284.9 %collective-permute-start = (bf16[128,7168]{1,0:T(8,128)(2,1)}, bf16[128,7168]{1,0:T(8,128)(2,1)S(1)}, u32[]{:S(2)}, u32[]{:S(2)}) collective-permute-start(bf16[128,7168]{1,0:T(8,128)(2,1)} %bitcast), channel_id=1, source_target_pairs={{32,0},{33,1},{34,2},{35,3},{36,4},{37,5},{38,6},{39,7},{40,8},{41... | collective-permute-start | bytes 5505032 | tf_op jit(solution)/shard_map/ppermute | solution.py:30
  46.4 72.4 %collective-permute-start.9 = (bf16[2,16,7168]{2,1,0:T(8,128)(2,1)}, bf16[2,16,7168]{2,1,0:T(8,128)(2,1)S(1)}, u32[]{:S(2)}, u32[]{:S(2)}) collective-permute-start(bf16[2,16,7168]{2,1,0:T(8,128)(2,1)} %collective-permute-done.2), channel_id=1, source_target_pairs={{0,1},{1,0},{2,3},{3,2},{4,5},{5,4},{6,7},{7,6},{8,9},{9,8},{10,11... | collective-permute-start | bytes 1376264 | tf_op jit(solution)/shard_map/ppermute | solution.py:23
  55.7 10.7 %collective-permute-start.4 = (bf16[2,16,7168]{2,1,0:T(8,128)(2,1)}, bf16[2,16,7168]{2,1,0:T(8,128)(2,1)S(1)}, u32[]{:S(2)}, u32[]{:S(2)}) collective-permute-start(bf16[2,16,7168]{2,1,0:T(8,128)(2,1)} %collective-permute-done.2), channel_id=1, source_target_pairs={{0,6},{1,7},{2,0},{3,1},{4,2},{5,3},{6,4},{7,5},{8,14},{9,15},{10,... | collective-permute-start | bytes 1376264 | tf_op jit(solution)/shard_map/ppermute | solution.py:23
  65.5 53.5 %collective-permute-start.36 = (bf16[2,16,7168]{2,1,0:T(8,128)(2,1)S(1)}, bf16[2,16,7168]{2,1,0:T(8,128)(2,1)S(1)}, u32[]{:S(2)}, u32[]{:S(2)}) collective-permute-start(bf16[2,16,7168]{2,1,0:T(8,128)(2,1)S(1)} %collective-permute-done.29), channel_id=1, source_target_pairs={{0,1},{1,0},{2,3},{3,2},{4,5},{5,4},{6,7},{7,6},{8,9},{9,8},{10,11... | collective-permute-start | bytes 1376264 | tf_op jit(solution)/shard_map/ppermute | solution.py:23
  66.4 9.0 %collective-permute-start.31 = (bf16[2,16,7168]{2,1,0:T(8,128)(2,1)S(1)}, bf16[2,16,7168]{2,1,0:T(8,128)(2,1)S(1)}, u32[]{:S(2)}, u32[]{:S(2)}) collective-permute-start(bf16[2,16,7168]{2,1,0:T(8,128)(2,1)S(1)} %collective-permute-done.29), channel_id=1, source_target_pairs={{0,6},{1,7},{2,0},{3,1},{4,2},{5,3},{6,4},{7,5},{8,14},{9,15},{10,... | collective-permute-start | bytes 1376264 | tf_op jit(solution)/shard_map/ppermute | solution.py:23
  67.2 33.6 %copy-start.9 = (bf16[16,16,7168]{2,1,0:T(8,128)(2,1)S(1)}, bf16[16,16,7168]{2,1,0:T(8,128)(2,1)}, u32[]{:S(2)}) copy-start(bf16[16,16,7168]{2,1,0:T(8,128)(2,1)} %get-tuple-element.71) | copy-start | bytes 11010052
  75.4 9.2 %collective-permute-start.32 = (bf16[2,16,7168]{2,1,0:T(8,128)(2,1)S(1)}, bf16[2,16,7168]{2,1,0:T(8,128)(2,1)S(1)}, u32[]{:S(2)}, u32[]{:S(2)}) collective-permute-start(bf16[2,16,7168]{2,1,0:T(8,128)(2,1)S(1)} %collective-permute-done.30), channel_id=1, source_target_pairs={{0,6},{1,7},{2,0},{3,1},{4,2},{5,3},{6,4},{7,5},{8,14},{9,15},{10,... | collective-permute-start | bytes 1376264 | tf_op jit(solution)/shard_map/ppermute | solution.py:23
  84.6 8.5 %collective-permute-start.13 = (bf16[2,16,7168]{2,1,0:T(8,128)(2,1)S(1)}, bf16[2,16,7168]{2,1,0:T(8,128)(2,1)S(1)}, u32[]{:S(2)}, u32[]{:S(2)}) collective-permute-start(bf16[2,16,7168]{2,1,0:T(8,128)(2,1)S(1)} %pad_maximum_fusion.10), channel_id=1, source_target_pairs={{0,2},{1,3},{2,4},{3,5},{4,6},{5,7},{6,0},{7,1},{8,10},{9,11},{10,... | collective-permute-start | bytes 1376264 | tf_op jit(solution)/shard_map/ppermute | solution.py:23
  93.2 7.6 %collective-permute-start.5 = (bf16[2,16,7168]{2,1,0:T(8,128)(2,1)S(1)}, bf16[2,16,7168]{2,1,0:T(8,128)(2,1)S(1)}, u32[]{:S(2)}, u32[]{:S(2)}) collective-permute-start(bf16[2,16,7168]{2,1,0:T(8,128)(2,1)S(1)} %pad_maximum_fusion.8), channel_id=1, source_target_pairs={{0,6},{1,7},{2,0},{3,1},{4,2},{5,3},{6,4},{7,5},{8,14},{9,15},{10,... | collective-permute-start | bytes 1376264 | tf_op jit(solution)/shard_map/ppermute | solution.py:23
  100.8 8.5 %collective-permute-start.41 = (bf16[2,16,7168]{2,1,0:T(8,128)(2,1)S(1)}, bf16[2,16,7168]{2,1,0:T(8,128)(2,1)S(1)}, u32[]{:S(2)}, u32[]{:S(2)}) collective-permute-start(bf16[2,16,7168]{2,1,0:T(8,128)(2,1)S(1)} %pad_maximum_fusion.16), channel_id=1, source_target_pairs={{0,2},{1,3},{2,4},{3,5},{4,6},{5,7},{6,0},{7,1},{8,10},{9,11},{10,... | collective-permute-start | bytes 1376264 | tf_op jit(solution)/shard_map/ppermute | solution.py:23
  109.3 7.6 %collective-permute-start.33 = (bf16[2,16,7168]{2,1,0:T(8,128)(2,1)S(1)}, bf16[2,16,7168]{2,1,0:T(8,128)(2,1)S(1)}, u32[]{:S(2)}, u32[]{:S(2)}) collective-permute-start(bf16[2,16,7168]{2,1,0:T(8,128)(2,1)S(1)} %pad_maximum_fusion.14), channel_id=1, source_target_pairs={{0,6},{1,7},{2,0},{3,1},{4,2},{5,3},{6,4},{7,5},{8,14},{9,15},{10,... | collective-permute-start | bytes 1376264 | tf_op jit(solution)/shard_map/ppermute | solution.py:23
  117.0 7.6 %collective-permute-start.37 = (bf16[2,16,7168]{2,1,0:T(8,128)(2,1)S(1)}, bf16[2,16,7168]{2,1,0:T(8,128)(2,1)S(1)}, u32[]{:S(2)}, u32[]{:S(2)}) collective-permute-start(bf16[2,16,7168]{2,1,0:T(8,128)(2,1)S(1)} %collective-permute-done.30), channel_id=1, source_target_pairs={{0,1},{1,0},{2,3},{3,2},{4,5},{5,4},{6,7},{7,6},{8,9},{9,8},{10,11... | collective-permute-start | bytes 1376264 | tf_op jit(solution)/shard_map/ppermute | solution.py:23
  117.1 12.1 %collective-permute-start.10 = (bf16[2,16,7168]{2,1,0:T(8,128)(2,1)S(1)}, bf16[2,16,7168]{2,1,0:T(8,128)(2,1)S(1)}, u32[]{:S(2)}, u32[]{:S(2)}) collective-permute-start(bf16[2,16,7168]{2,1,0:T(8,128)(2,1)S(1)} %pad_maximum_fusion.8), channel_id=1, source_target_pairs={{0,1},{1,0},{2,3},{3,2},{4,5},{5,4},{6,7},{7,6},{8,9},{9,8},{10,11... | collective-permute-start | bytes 1376264 | tf_op jit(solution)/shard_map/ppermute | solution.py:23
  118.8 18.1 %collective-permute-start.38 = (bf16[2,16,7168]{2,1,0:T(8,128)(2,1)S(1)}, bf16[2,16,7168]{2,1,0:T(8,128)(2,1)S(1)}, u32[]{:S(2)}, u32[]{:S(2)}) collective-permute-start(bf16[2,16,7168]{2,1,0:T(8,128)(2,1)S(1)} %pad_maximum_fusion.14), channel_id=1, source_target_pairs={{0,1},{1,0},{2,3},{3,2},{4,5},{5,4},{6,7},{7,6},{8,9},{9,8},{10,11... | collective-permute-start | bytes 1376264 | tf_op jit(solution)/shard_map/ppermute | solution.py:23
  119.0 42.0 %collective-permute-start.15 = (bf16[2,16,7168]{2,1,0:T(8,128)(2,1)S(1)}, bf16[2,16,7168]{2,1,0:T(8,128)(2,1)S(1)}, u32[]{:S(2)}, u32[]{:S(2)}) collective-permute-start(bf16[2,16,7168]{2,1,0:T(8,128)(2,1)S(1)} %pad_maximum_fusion.11), channel_id=1, source_target_pairs={{0,2},{1,3},{2,4},{3,5},{4,6},{5,7},{6,0},{7,1},{8,10},{9,11},{10,... | collective-permute-start | bytes 1376264 | tf_op jit(solution)/shard_map/ppermute | solution.py:23
  124.6 14.2 %collective-permute-start.14 = (bf16[2,16,7168]{2,1,0:T(8,128)(2,1)S(1)}, bf16[2,16,7168]{2,1,0:T(8,128)(2,1)S(1)}, u32[]{:S(2)}, u32[]{:S(2)}) collective-permute-start(bf16[2,16,7168]{2,1,0:T(8,128)(2,1)S(1)} %pad_maximum_fusion.11), channel_id=1, source_target_pairs={{0,6},{1,7},{2,0},{3,1},{4,2},{5,3},{6,4},{7,5},{8,14},{9,15},{10,... | collective-permute-start | bytes 1376264 | tf_op jit(solution)/shard_map/ppermute | solution.py:23
  129.2 61.1 %collective-permute-start.44 = (bf16[2,16,7168]{2,1,0:T(8,128)(2,1)S(1)}, bf16[2,16,7168]{2,1,0:T(8,128)(2,1)S(1)}, u32[]{:S(2)}, u32[]{:S(2)}) collective-permute-start(bf16[2,16,7168]{2,1,0:T(8,128)(2,1)S(1)} %pad_maximum_fusion.17), channel_id=1, source_target_pairs={{0,2},{1,3},{2,4},{3,5},{4,6},{5,7},{6,0},{7,1},{8,10},{9,11},{10,... | collective-permute-start | bytes 1376264 | tf_op jit(solution)/shard_map/ppermute | solution.py:23
  136.9 22.9 %collective-permute-start.42 = (bf16[2,16,7168]{2,1,0:T(8,128)(2,1)S(1)}, bf16[2,16,7168]{2,1,0:T(8,128)(2,1)S(1)}, u32[]{:S(2)}, u32[]{:S(2)}) collective-permute-start(bf16[2,16,7168]{2,1,0:T(8,128)(2,1)S(1)} %pad_maximum_fusion.17), channel_id=1, source_target_pairs={{0,6},{1,7},{2,0},{3,1},{4,2},{5,3},{6,4},{7,5},{8,14},{9,15},{10,... | collective-permute-start | bytes 1376264 | tf_op jit(solution)/shard_map/ppermute | solution.py:23
  138.8 12.9 %collective-permute-start.11 = (bf16[2,16,7168]{2,1,0:T(8,128)(2,1)S(1)}, bf16[2,16,7168]{2,1,0:T(8,128)(2,1)S(1)}, u32[]{:S(2)}, u32[]{:S(2)}) collective-permute-start(bf16[2,16,7168]{2,1,0:T(8,128)(2,1)S(1)} %collective-permute-done.5), channel_id=1, source_target_pairs={{0,1},{1,0},{2,3},{3,2},{4,5},{5,4},{6,7},{7,6},{8,9},{9,8},{10,11... | collective-permute-start | bytes 1376264 | tf_op jit(solution)/shard_map/ppermute | solution.py:23
  139.5 47.2 %copy-start.2 = (bf16[1,1,7168,256]{3,2,1,0:T(8,128)(2,1)S(1)}, bf16[1,1,7168,256]{3,2,1,0:T(8,128)(2,1)}, u32[]{:S(2)}) copy-start(bf16[1,1,7168,256]{3,2,1,0:T(8,128)(2,1)} %param.12) | copy-start | bytes 11010052
  151.8 7.6 %collective-permute-start.12 = (bf16[2,16,7168]{2,1,0:T(8,128)(2,1)S(1)}, bf16[2,16,7168]{2,1,0:T(8,128)(2,1)S(1)}, u32[]{:S(2)}, u32[]{:S(2)}) collective-permute-start(bf16[2,16,7168]{2,1,0:T(8,128)(2,1)S(1)} %pad_maximum_fusion.9), channel_id=1, source_target_pairs={{0,1},{1,0},{2,3},{3,2},{4,5},{5,4},{6,7},{7,6},{8,9},{9,8},{10,11... | collective-permute-start | bytes 1376264 | tf_op jit(solution)/shard_map/ppermute | solution.py:23
  159.4 18.7 %collective-permute-start.40 = (bf16[2,16,7168]{2,1,0:T(8,128)(2,1)S(1)}, bf16[2,16,7168]{2,1,0:T(8,128)(2,1)S(1)}, u32[]{:S(2)}, u32[]{:S(2)}) collective-permute-start(bf16[2,16,7168]{2,1,0:T(8,128)(2,1)S(1)} %pad_maximum_fusion.15), channel_id=1, source_target_pairs={{0,1},{1,0},{2,3},{3,2},{4,5},{5,4},{6,7},{7,6},{8,9},{9,8},{10,11... | collective-permute-start | bytes 1376264 | tf_op jit(solution)/shard_map/ppermute | solution.py:23
  159.7 18.3 %collective-permute-start.39 = (bf16[2,16,7168]{2,1,0:T(8,128)(2,1)S(1)}, bf16[2,16,7168]{2,1,0:T(8,128)(2,1)S(1)}, u32[]{:S(2)}, u32[]{:S(2)}) collective-permute-start(bf16[2,16,7168]{2,1,0:T(8,128)(2,1)S(1)} %collective-permute-done.33), channel_id=1, source_target_pairs={{0,1},{1,0},{2,3},{3,2},{4,5},{5,4},{6,7},{7,6},{8,9},{9,8},{10,11... | collective-permute-start | bytes 1376264 | tf_op jit(solution)/shard_map/ppermute | solution.py:23
  161.0 27.3 %collective-permute-start.43 = (bf16[2,16,7168]{2,1,0:T(8,128)(2,1)S(1)}, bf16[2,16,7168]{2,1,0:T(8,128)(2,1)S(1)}, u32[]{:S(2)}, u32[]{:S(2)}) collective-permute-start(bf16[2,16,7168]{2,1,0:T(8,128)(2,1)S(1)} %collective-permute-done.42), channel_id=1, source_target_pairs={{0,6},{1,7},{2,0},{3,1},{4,2},{5,3},{6,4},{7,5},{8,14},{9,15},{10,... | collective-permute-start | bytes 1376264 | tf_op jit(solution)/shard_map/ppermute | solution.py:23
  178.0 8.5 %collective-permute-start.16 = (bf16[2,16,7168]{2,1,0:T(8,128)(2,1)S(1)}, bf16[2,16,7168]{2,1,0:T(8,128)(2,1)S(1)}, u32[]{:S(2)}, u32[]{:S(2)}) collective-permute-start(bf16[2,16,7168]{2,1,0:T(8,128)(2,1)S(1)} %collective-permute-done.15), channel_id=1, source_target_pairs={{0,2},{1,3},{2,4},{3,5},{4,6},{5,7},{6,0},{7,1},{8,10},{9,11},{10,... | collective-permute-start | bytes 1376264 | tf_op jit(solution)/shard_map/ppermute | solution.py:23
  214.8 6.2 %collective-permute-start.17 = (bf16[16,7296]{1,0:T(8,128)(2,1)S(1)}, bf16[16,7296]{1,0:T(8,128)(2,1)S(1)}, u32[]{:S(2)}, u32[]{:S(2)}) collective-permute-start(bf16[16,7296]{1,0:T(8,128)(2,1)S(1)} %get-tuple-element.22), channel_id=1, source_target_pairs={{0,2},{1,3},{2,4},{3,5},{4,6},{5,7},{6,0},{7,1},{8,10},{9,11},{10,... | collective-permute-start | bytes 700424 | tf_op jit(solution)/shard_map/ppermute | solution.py:23
  214.9 6.1 %collective-permute-start.19 = (bf16[16,7296]{1,0:T(8,128)(2,1)S(1)}, bf16[16,7296]{1,0:T(8,128)(2,1)S(1)}, u32[]{:S(2)}, u32[]{:S(2)}) collective-permute-start(bf16[16,7296]{1,0:T(8,128)(2,1)S(1)} %get-tuple-element.23), channel_id=1, source_target_pairs={{0,6},{1,7},{2,0},{3,1},{4,2},{5,3},{6,4},{7,5},{8,14},{9,15},{10,... | collective-permute-start | bytes 700424 | tf_op jit(solution)/shard_map/ppermute | solution.py:23
  217.6 12.4 %collective-permute-start.23 = (bf16[4,16,7296]{2,1,0:T(8,128)(2,1)S(1)}, bf16[4,16,7296]{2,1,0:T(8,128)(2,1)S(1)}, u32[]{:S(2)}, u32[]{:S(2)}) collective-permute-start(bf16[4,16,7296]{2,1,0:T(8,128)(2,1)S(1)} %slice_bitcast_fusion.1), channel_id=1, source_target_pairs={{0,1},{1,0},{2,3},{3,2},{4,5},{5,4},{6,7},{7,6},{8,9},{9,8},{10,11... | collective-permute-start | bytes 2801672 | tf_op jit(solution)/shard_map/ppermute | solution.py:23
  217.7 12.9 %collective-permute-start.45 = (bf16[16,7296]{1,0:T(8,128)(2,1)S(1)}, bf16[16,7296]{1,0:T(8,128)(2,1)S(1)}, u32[]{:S(2)}, u32[]{:S(2)}) collective-permute-start(bf16[16,7296]{1,0:T(8,128)(2,1)S(1)} %get-tuple-element.14), channel_id=1, source_target_pairs={{0,2},{1,3},{2,4},{3,5},{4,6},{5,7},{6,0},{7,1},{8,10},{9,11},{10,... | collective-permute-start | bytes 700424 | tf_op jit(solution)/shard_map/ppermute | solution.py:23
  221.0 12.2 %collective-permute-start.47 = (bf16[16,7296]{1,0:T(8,128)(2,1)S(1)}, bf16[16,7296]{1,0:T(8,128)(2,1)S(1)}, u32[]{:S(2)}, u32[]{:S(2)}) collective-permute-start(bf16[16,7296]{1,0:T(8,128)(2,1)S(1)} %get-tuple-element.15), channel_id=1, source_target_pairs={{0,6},{1,7},{2,0},{3,1},{4,2},{5,3},{6,4},{7,5},{8,14},{9,15},{10,... | collective-permute-start | bytes 700424 | tf_op jit(solution)/shard_map/ppermute | solution.py:23
  221.1 19.5 %collective-permute-start.51 = (bf16[4,16,7296]{2,1,0:T(8,128)(2,1)S(1)}, bf16[4,16,7296]{2,1,0:T(8,128)(2,1)S(1)}, u32[]{:S(2)}, u32[]{:S(2)}) collective-permute-start(bf16[4,16,7296]{2,1,0:T(8,128)(2,1)S(1)} %slice_bitcast_fusion), channel_id=1, source_target_pairs={{0,1},{1,0},{2,3},{3,2},{4,5},{5,4},{6,7},{7,6},{8,9},{9,8},{10,11... | collective-permute-start | bytes 2801672 | tf_op jit(solution)/shard_map/ppermute | solution.py:23
  230.4 10.9 %collective-permute-start.24 = (bf16[8,7296]{1,0:T(8,128)(2,1)S(1)}, bf16[8,7296]{1,0:T(8,128)(2,1)S(1)}, u32[]{:S(2)}, u32[]{:S(2)}) collective-permute-start(bf16[8,7296]{1,0:T(8,128)(2,1)S(1)} %get-tuple-element.80), channel_id=1, source_target_pairs={{0,2},{1,3},{2,4},{3,5},{4,6},{5,7},{6,0},{7,1},{8,10},{9,11},{10,... | collective-permute-start | bytes 350216 | tf_op jit(solution)/shard_map/ppermute | solution.py:23
  230.6 12.1 %collective-permute-start.26 = (bf16[8,7296]{1,0:T(8,128)(2,1)S(1)}, bf16[8,7296]{1,0:T(8,128)(2,1)S(1)}, u32[]{:S(2)}, u32[]{:S(2)}) collective-permute-start(bf16[8,7296]{1,0:T(8,128)(2,1)S(1)} %get-tuple-element.81), channel_id=1, source_target_pairs={{0,6},{1,7},{2,0},{3,1},{4,2},{5,3},{6,4},{7,5},{8,14},{9,15},{10,... | collective-permute-start | bytes 350216 | tf_op jit(solution)/shard_map/ppermute | solution.py:23
  233.3 26.3 %collective-permute-start.18 = (bf16[2,16,7296]{2,1,0:T(8,128)(2,1)S(1)}, bf16[2,16,7296]{2,1,0:T(8,128)(2,1)S(1)}, u32[]{:S(2)}, u32[]{:S(2)}) collective-permute-start(bf16[2,16,7296]{2,1,0:T(8,128)(2,1)S(1)} %pad_maximum_fusion.2), channel_id=1, source_target_pairs={{0,2},{1,3},{2,4},{3,5},{4,6},{5,7},{6,0},{7,1},{8,10},{9,11},{10,... | collective-permute-start | bytes 1400840 | tf_op jit(solution)/shard_map/ppermute | solution.py:23
  240.5 20.2 %collective-permute-start.20 = (bf16[2,16,7296]{2,1,0:T(8,128)(2,1)S(1)}, bf16[2,16,7296]{2,1,0:T(8,128)(2,1)S(1)}, u32[]{:S(2)}, u32[]{:S(2)}) collective-permute-start(bf16[2,16,7296]{2,1,0:T(8,128)(2,1)S(1)} %pad_maximum_fusion.3), channel_id=1, source_target_pairs={{0,6},{1,7},{2,0},{3,1},{4,2},{5,3},{6,4},{7,5},{8,14},{9,15},{10,... | collective-permute-start | bytes 1400840 | tf_op jit(solution)/shard_map/ppermute | solution.py:23
  241.4 6.8 %collective-permute-start.52 = (bf16[8,7296]{1,0:T(8,128)(2,1)S(1)}, bf16[8,7296]{1,0:T(8,128)(2,1)S(1)}, u32[]{:S(2)}, u32[]{:S(2)}) collective-permute-start(bf16[8,7296]{1,0:T(8,128)(2,1)S(1)} %get-tuple-element.78), channel_id=1, source_target_pairs={{0,2},{1,3},{2,4},{3,5},{4,6},{5,7},{6,0},{7,1},{8,10},{9,11},{10,... | collective-permute-start | bytes 350216 | tf_op jit(solution)/shard_map/ppermute | solution.py:23
  242.7 9.3 %collective-permute-start.54 = (bf16[8,7296]{1,0:T(8,128)(2,1)S(1)}, bf16[8,7296]{1,0:T(8,128)(2,1)S(1)}, u32[]{:S(2)}, u32[]{:S(2)}) collective-permute-start(bf16[8,7296]{1,0:T(8,128)(2,1)S(1)} %get-tuple-element.79), channel_id=1, source_target_pairs={{0,6},{1,7},{2,0},{3,1},{4,2},{5,3},{6,4},{7,5},{8,14},{9,15},{10,... | collective-permute-start | bytes 350216 | tf_op jit(solution)/shard_map/ppermute | solution.py:23
  248.2 6.3 %collective-permute-start.27 = (bf16[16,7296]{1,0:T(8,128)(2,1)S(1)}, bf16[16,7296]{1,0:T(8,128)(2,1)S(1)}, u32[]{:S(2)}, u32[]{:S(2)}) collective-permute-start(bf16[16,7296]{1,0:T(8,128)(2,1)S(1)} %pad_maximum_fusion.19), channel_id=1, source_target_pairs={{0,6},{1,7},{2,0},{3,1},{4,2},{5,3},{6,4},{7,5},{8,14},{9,15},{10,... | collective-permute-start | bytes 700424 | tf_op jit(solution)/shard_map/ppermute | solution.py:23
  252.0 7.6 %collective-permute-start.25 = (bf16[16,7296]{1,0:T(8,128)(2,1)S(1)}, bf16[16,7296]{1,0:T(8,128)(2,1)S(1)}, u32[]{:S(2)}, u32[]{:S(2)}) collective-permute-start(bf16[16,7296]{1,0:T(8,128)(2,1)S(1)} %pad_maximum_fusion.18), channel_id=1, source_target_pairs={{0,2},{1,3},{2,4},{3,5},{4,6},{5,7},{6,0},{7,1},{8,10},{9,11},{10,... | collective-permute-start | bytes 700424 | tf_op jit(solution)/shard_map/ppermute | solution.py:23
  254.5 21.2 %collective-permute-start.46 = (bf16[2,16,7296]{2,1,0:T(8,128)(2,1)S(1)}, bf16[2,16,7296]{2,1,0:T(8,128)(2,1)S(1)}, u32[]{:S(2)}, u32[]{:S(2)}) collective-permute-start(bf16[2,16,7296]{2,1,0:T(8,128)(2,1)S(1)} %pad_maximum_fusion.4), channel_id=1, source_target_pairs={{0,2},{1,3},{2,4},{3,5},{4,6},{5,7},{6,0},{7,1},{8,10},{9,11},{10,... | collective-permute-start | bytes 1400840 | tf_op jit(solution)/shard_map/ppermute | solution.py:23
  259.6 16.1 %collective-permute-start.48 = (bf16[2,16,7296]{2,1,0:T(8,128)(2,1)S(1)}, bf16[2,16,7296]{2,1,0:T(8,128)(2,1)S(1)}, u32[]{:S(2)}, u32[]{:S(2)}) collective-permute-start(bf16[2,16,7296]{2,1,0:T(8,128)(2,1)S(1)} %pad_maximum_fusion.5), channel_id=1, source_target_pairs={{0,6},{1,7},{2,0},{3,1},{4,2},{5,3},{6,4},{7,5},{8,14},{9,15},{10,... | collective-permute-start | bytes 1400840 | tf_op jit(solution)/shard_map/ppermute | solution.py:23
  259.6 16.1 %collective-permute-start.55 = (bf16[16,7296]{1,0:T(8,128)(2,1)S(1)}, bf16[16,7296]{1,0:T(8,128)(2,1)S(1)}, u32[]{:S(2)}, u32[]{:S(2)}) collective-permute-start(bf16[16,7296]{1,0:T(8,128)(2,1)S(1)} %pad_maximum_fusion.21), channel_id=1, source_target_pairs={{0,6},{1,7},{2,0},{3,1},{4,2},{5,3},{6,4},{7,5},{8,14},{9,15},{10,... | collective-permute-start | bytes 700424 | tf_op jit(solution)/shard_map/ppermute | solution.py:23
  260.7 15.0 %collective-permute-start.53 = (bf16[16,7296]{1,0:T(8,128)(2,1)S(1)}, bf16[16,7296]{1,0:T(8,128)(2,1)S(1)}, u32[]{:S(2)}, u32[]{:S(2)}) collective-permute-start(bf16[16,7296]{1,0:T(8,128)(2,1)S(1)} %pad_maximum_fusion.20), channel_id=1, source_target_pairs={{0,2},{1,3},{2,4},{3,5},{4,6},{5,7},{6,0},{7,1},{8,10},{9,11},{10,... | collective-permute-start | bytes 700424 | tf_op jit(solution)/shard_map/ppermute | solution.py:23
  261.4 50.7 %copy-start.6 = (s32[1,128,8]{1,2,0:T(8,128)S(1)}, s32[1,128,8]{1,2,0:T(8,128)}, u32[]{:S(2)}) copy-start(s32[1,128,8]{1,2,0:T(8,128)} %param.10) | copy-start | bytes 12292
  261.4 50.7 %copy-start.10 = (f32[1,128,8]{1,2,0:T(8,128)S(1)}, f32[1,128,8]{1,2,0:T(8,128)}, u32[]{:S(2)}) copy-start(f32[1,128,8]{1,2,0:T(8,128)} %param.11) | copy-start | bytes 12292
  275.7 5.2 %collective-permute-start.21 = (bf16[16,7296]{1,0:T(8,128)(2,1)S(1)}, bf16[16,7296]{1,0:T(8,128)(2,1)S(1)}, u32[]{:S(2)}, u32[]{:S(2)}) collective-permute-start(bf16[16,7296]{1,0:T(8,128)(2,1)S(1)} %get-tuple-element.19), channel_id=1, source_target_pairs={{0,1},{1,0},{2,3},{3,2},{4,5},{5,4},{6,7},{7,6},{8,9},{9,8},{10,11... | collective-permute-start | bytes 700424 | tf_op jit(solution)/shard_map/ppermute | solution.py:23
  276.0 27.8 %collective-permute-start.57 = (bf16[16,128]{1,0:T(8,128)(2,1)S(1)}, bf16[16,128]{1,0:T(8,128)(2,1)S(1)}, u32[]{:S(2)}, u32[]{:S(2)}) collective-permute-start(bf16[16,128]{1,0:T(8,128)(2,1)S(1)} %slice.497), channel_id=1, source_target_pairs={{0,24},{1,25},{2,26},{3,27},{4,28},{5,29},{6,30},{7,31},{8,0},{9,1... | collective-permute-start | bytes 12296 | tf_op jit(solution)/shard_map/ppermute | solution.py:23
  276.1 31.9 %collective-permute-start.59 = (bf16[16,128]{1,0:T(8,128)(2,1)S(1)}, bf16[16,128]{1,0:T(8,128)(2,1)S(1)}, u32[]{:S(2)}, u32[]{:S(2)}) collective-permute-start(bf16[16,128]{1,0:T(8,128)(2,1)S(1)} %slice.499), channel_id=1, source_target_pairs={{0,8},{1,9},{2,10},{3,11},{4,12},{5,13},{6,14},{7,15},{8,16},{9,17... | collective-permute-start | bytes 12296 | tf_op jit(solution)/shard_map/ppermute | solution.py:23
  277.5 25.4 %collective-permute-start.49 = (bf16[16,7296]{1,0:T(8,128)(2,1)S(1)}, bf16[16,7296]{1,0:T(8,128)(2,1)S(1)}, u32[]{:S(2)}, u32[]{:S(2)}) collective-permute-start(bf16[16,7296]{1,0:T(8,128)(2,1)S(1)} %get-tuple-element.11), channel_id=1, source_target_pairs={{0,1},{1,0},{2,3},{3,2},{4,5},{5,4},{6,7},{7,6},{8,9},{9,8},{10,11... | collective-permute-start | bytes 700424 | tf_op jit(solution)/shard_map/ppermute | solution.py:23
  281.1 31.8 %collective-permute-start.22 = (bf16[16,7168]{1,0:T(8,128)(2,1)S(1)}, bf16[16,7168]{1,0:T(8,128)(2,1)S(1)}, u32[]{:S(2)}, u32[]{:S(2)}) collective-permute-start(bf16[16,7168]{1,0:T(8,128)(2,1)S(1)} %slice.430), channel_id=1, source_target_pairs={{32,0},{33,1},{34,2},{35,3},{36,4},{37,5},{38,6},{39,7},{40,8},{41... | collective-permute-start | bytes 688136 | tf_op jit(solution)/shard_map/ppermute | solution.py:30
  303.1 6.8 %collective-permute-start.58 = (bf16[16,128]{1,0:T(8,128)(2,1)S(1)}, bf16[16,128]{1,0:T(8,128)(2,1)S(1)}, u32[]{:S(2)}, u32[]{:S(2)}) collective-permute-start(bf16[16,128]{1,0:T(8,128)(2,1)S(1)} %slice.498), channel_id=1, source_target_pairs={{0,16},{1,17},{2,18},{3,19},{4,20},{5,21},{6,22},{7,23},{8,24},{9,... | collective-permute-start | bytes 12296 | tf_op jit(solution)/shard_map/ppermute | solution.py:23
  303.9 12.4 %collective-permute-start.28 = (bf16[16,7168]{1,0:T(8,128)(2,1)S(1)}, bf16[16,7168]{1,0:T(8,128)(2,1)S(1)}, u32[]{:S(2)}, u32[]{:S(2)}) collective-permute-start(bf16[16,7168]{1,0:T(8,128)(2,1)S(1)} %slice.446), channel_id=1, source_target_pairs={{32,24},{33,25},{34,26},{35,27},{36,28},{37,29},{38,30},{39,31},{4... | collective-permute-start | bytes 688136 | tf_op jit(solution)/shard_map/ppermute | solution.py:30
  308.0 17.0 %collective-permute-start.56 = (bf16[16,7168]{1,0:T(8,128)(2,1)S(1)}, bf16[16,7168]{1,0:T(8,128)(2,1)S(1)}, u32[]{:S(2)}, u32[]{:S(2)}) collective-permute-start(bf16[16,7168]{1,0:T(8,128)(2,1)S(1)} %slice.495), channel_id=1, source_target_pairs={{32,8},{33,9},{34,10},{35,11},{36,12},{37,13},{38,14},{39,15},{40,... | collective-permute-start | bytes 688136 | tf_op jit(solution)/shard_map/ppermute | solution.py:30
  310.0 15.1 %collective-permute-start.50 = (bf16[16,7168]{1,0:T(8,128)(2,1)S(1)}, bf16[16,7168]{1,0:T(8,128)(2,1)S(1)}, u32[]{:S(2)}, u32[]{:S(2)}) collective-permute-start(bf16[16,7168]{1,0:T(8,128)(2,1)S(1)} %slice.479), channel_id=1, source_target_pairs={{32,16},{33,17},{34,18},{35,19},{36,20},{37,21},{38,22},{39,23},{4... | collective-permute-start | bytes 688136 | tf_op jit(solution)/shard_map/ppermute | solution.py:30
  312.9 12.3 %collective-permute-start.1 = (f32[128,64]{0,1:T(8,128)S(1)}, f32[128,64]{0,1:T(8,128)S(1)}, u32[]{:S(2)}, u32[]{:S(2)}) collective-permute-start(f32[128,64]{0,1:T(8,128)S(1)} %bitcast_select_fusion), channel_id=1, source_target_pairs={{32,0},{33,1},{34,2},{35,3},{36,4},{37,5},{38,6},{39,7},{40,8},{41... | collective-permute-start | bytes 98312 | tf_op jit(solution)/shard_map/ppermute | solution.py:30
  (8 other events, 69.3 us)
